TPU v7x, 32 devices: a whole 2x2x4 slice. The times are simulated.
32 devices in a mesh: row: 16 (over z, y, core), col: 2 (over x).
Axes of the slice: x: 2, y: 2, z: 4, core: 2. Of those that a mesh axis runs over, the one named last changes fastest.
Arguments:
- activations: bfloat16 [2, 512, 14848], P(None, 'row', 'col'), may hold values from -6 to 6
- output_gradient: bfloat16 [2, 512, 29696], P(None, 'col', 'row'), may hold values from -4 to 4
- weight: bfloat16 [14848, 29696], P('col', 'row'), may hold values from -0.046875 to 0.046875
Outputs:
- fisher: float32 [14848, 29696], P('col', 'row')
- activation_gradient: bfloat16 [2, 512, 14848], P(None, 'row', 'col')
All inputs are finite; a program needn't handle non-finite values.
Results may differ from a plain program's by a relative error of at most 0.001.
Values may be sent and summed in bfloat16 or wider, within the bound.
A program may use at most 256 MiB of HBM per device.

v0:
```python
import jax
import jax.numpy as jnp
from jax import lax
from jax.sharding import PartitionSpec as P


def local(activations, output_gradient, weight):
    seqs = activations.shape[0]
    gradient_everything = lax.all_gather(output_gradient, "col", axis=1, tiled=True)
    length = gradient_everything.shape[1]
    input_gathered = lax.all_gather(activations, "row", axis=1, tiled=True)
    gradient_list = jnp.einsum(
        "qkc,qkh->qch", input_gathered, gradient_everything, preferred_element_type=jnp.float32
    )
    fisher = jnp.sum(gradient_list * gradient_list, axis=0) / (seqs * length)
    partial_totals = jnp.einsum(
        "gkw,xw->gkx", gradient_everything, weight, preferred_element_type=jnp.float32
    )
    activation_gradient = lax.psum_scatter(partial_totals, "row", scatter_dimension=1, tiled=True)
    return (fisher, activation_gradient.astype(jnp.bfloat16))


def solution(mesh):
    return jax.shard_map(
        local,
        mesh=mesh,
        in_specs=(P(None, "row", "col"), P(None, "col", "row"), P("col", "row")),
        out_specs=(P("col", "row"), P(None, "row", "col")),
        check_vma=False,
    )
```

profile of v0, /device:TPU:0, one launch (start us, length us, event | category | flops | bytes accessed | tf_op | source)
XLA Modules:
  0.0 481.7 jit_solution(257428681788821069)
XLA Ops:
  7.2 0.0 all-gather.5.cloned.1.call-start
  7.2 0.7 all-gather.5.cloned.1.call-update
  7.9 0.0 all-gather.3.cloned.1.call-start
  7.9 0.7 all-gather.3.cloned.1.call-update
  8.6 0.0 reduce-scatter.2.cloned.1.call-start
  8.7 55.9 %all-gather.5.cloned.1.call-done = bf16[2,512,1856]{1,2,0:T(8,128)(2,1)} async-done(((bf16[2,256,1856]{1,2,0:T(8,128)(2,1)}), bf16[2,512,1856]{1,2,0:T(8,128)(2,1)}) %all-gather.5.cloned.1.call-update) | async-done | bytes 3801104 | tf_op jit(solution)/shard_map/all_gather | solution.py:9
  64.5 39.8 %fusion = f32[2,512,7424]{2,1,0:T(8,128)} fusion(bf16[2,512,1856]{1,2,0:T(8,128)(2,1)} %all-gather.5.cloned.1.call-done, bf16[7424,1856]{0,1:T(8,128)(2,1)} %param.5), kind=kOutput, calls=%fused_computation.1 | convolution fusion | flops 28219277312 | bytes 61767680 | tf_op jit(solution)/shard_map/gkw,xw->gkx/dot_general | solution.py:16
  104.4 0.0 reduce-scatter.2.cloned.1.call-update
  104.4 79.6 %all-gather.3.cloned.1.call-done = bf16[2,512,7424]{2,1,0:T(8,128)(2,1)} async-done(((bf16[2,32,7424]{2,1,0:T(8,128)(2,1)}), bf16[2,512,7424]{2,1,0:T(8,128)(2,1)}) %all-gather.3.cloned.1.call-update) | async-done | bytes 15204368 | tf_op jit(solution)/shard_map/all_gather | solution.py:11
  184.0 72.8 %multiply_reduce_fusion = f32[7424,1856]{0,1:T(8,128)} fusion(bf16[2,512,1856]{1,2,0:T(8,128)(2,1)} %all-gather.5.cloned.1.call-done, bf16[2,512,7424]{2,1,0:T(8,128)(2,1)} %all-gather.3.cloned.1.call-done), kind=kOutput, calls=%fused_computation | convolution fusion | flops 28260614144 | bytes 74121216 | tf_op jit(solution)/shard_map/qkc,qkh->qch/dot_general | solution.py:12
  256.8 37.4 %broadcast_multiply_fusion = f32[7424,1856]{0,1:T(8,128)} fusion(f32[7424,1856]{0,1:T(8,128)} %multiply_reduce_fusion), kind=kLoop, calls=%fused_computation.3 | loop fusion | flops 13778944 | bytes 110231552 | tf_op jit(solution)/shard_map/div | solution.py:15
  294.2 178.5 %reduce-scatter.2.cloned.1.call-done = f32[2,32,7424]{2,1,0:T(8,128)} async-done(((f32[2,512,7424]{2,1,0:T(8,128)}), f32[2,32,7424]{2,1,0:T(8,128)}) %reduce-scatter.2.cloned.1.call-update) | async-done | bytes 1900560 | tf_op jit(solution)/shard_map/reduce_scatter | solution.py:19
  472.7 2.6 convert_element_type.3
Async XLA Ops:
  7.2 57.4 %all-gather.5.cloned.1.call-start = ((), (), s32[]{:S(2)}) async-start(), calls=%async_computation.2 | async-start | bytes 5701632 | tf_op jit(solution)/shard_map/all_gather | solution.py:9
  7.9 176.1 %all-gather.3.cloned.1.call-start = ((), (), s32[]{:S(2)}) async-start(), calls=%async_computation.1 | async-start | bytes 16154624 | tf_op jit(solution)/shard_map/all_gather | solution.py:11
  8.6 464.0 %reduce-scatter.2.cloned.1.call-start = ((), (), s32[]{:S(2)}) async-start(), calls=%async_computation.3 | async-start | bytes 32309248 | tf_op jit(solution)/shard_map/reduce_scatter | solution.py:19
Sparse Core Ops, SparseCore 0:
  9.5 54.9 all-gather.4
  66.8 117.0 all-gather.2
  188.2 284.4 reduce-scatter.1
where the time goes:
time: 482 us
  waiting for transfers between devices  315 us (65%)
  matrix products  113 us (23%)
  other arithmetic  39.9 us (8%)
  between operations  13.7 us (3%)
    reduce_scatter x1, waiting for transfers between devices, local(): lax.psum_scatter(partial_totals, 'row', scatter_dimension=1, tiled=True)  178 us
    all_gather x1, waiting for transfers between devices, local(): input_gathered = lax.all_gather(activations, 'row', axis=1, tiled=True)  79.6 us
    dot_general x1, matrix products, local(): jnp.einsum('qkc,qkh->qch', input_gathered, gradient_everything, preferred...  72.8 us
    all_gather x1, waiting for transfers between devices, local(): lax.all_gather(output_gradient, 'col', axis=1, tiled=True)  55.9 us
    dot_general x1, matrix products, local(): jnp.einsum('gkw,xw->gkx', gradient_everything, weight, preferred_element_...  39.8 us
    div x1, other arithmetic, local(): fisher = jnp.sum(gradient_list * gradient_list, axis=0) / (seqs * length)  37.4 us
  transfers between devices with their start and end apart: 3, of which 3 were waited for; matrix products, arithmetic and copies ran while one was open for 31% of the time, Pallas kernels for 0%

commit v1 on v0

v1 whole, which is shorter than its diff:
```python
import jax
import jax.numpy as jnp
from jax import lax
from jax.experimental import pallas as pl
from jax.experimental.pallas import tpu as pltpu
from jax.sharding import PartitionSpec as P

SHARES = (6, 12, 17, 22, 26, 29)


def fisher_kernel(scale, g_ref, a_ref, o_ref):
    hidden = g_ref.shape[1]
    steps = next(n for n in (4, 2, 1) if hidden % (16 * n) == 0)
    rows = hidden // steps
    for i in range(steps):
        at = pl.ds(i * rows, rows)
        total = None
        for s in range(g_ref.shape[0]):
            grad = jnp.dot(g_ref[s, at, :], a_ref[s], preferred_element_type=jnp.float32)
            total = grad * grad if total is None else total + grad * grad
        o_ref[at, :] = total * scale


def fisher_of(g_t, act):
    seqs, hidden, length = g_t.shape
    width = act.shape[2]
    tile = 256 if width % 256 == 0 else width
    return pl.pallas_call(
        lambda *refs: fisher_kernel(1.0 / (seqs * length), *refs),
        grid=(width // tile,),
        in_specs=[
            pl.BlockSpec((seqs, hidden, length), lambda i: (0, 0, 0)),
            pl.BlockSpec((seqs, length, tile), lambda i: (0, 0, i)),
        ],
        out_specs=pl.BlockSpec((hidden, tile), lambda i: (0, i)),
        out_shape=jax.ShapeDtypeStruct((hidden, width), jnp.float32),
        cost_estimate=pl.CostEstimate(
            flops=2 * seqs * hidden * length * width,
            bytes_accessed=4 * hidden * width + 2 * seqs * length * (hidden + width),
            transcendentals=0,
        ),
        compiler_params=pltpu.CompilerParams(vmem_limit_bytes=48 * 2**20),
    )(g_t, act)


def cuts(width):
    unit = 256 if width % 256 == 0 else width
    count = width // unit
    edges = [0] + [unit * (count * n // SHARES[-1]) for n in SHARES]
    return [(low, high) for low, high in zip(edges[:-1], edges[1:]) if high > low], unit


def reduce_kernel(line, groups, pieces, unit, rows_ref, w_hbm, *refs):
    if groups == 2:
        g_hbm, out_ref, g_other_hbm, *scratch = refs
    else:
        out_ref, *scratch = refs
    count = len(pieces)
    held = scratch[:count]
    from_y = scratch[count : 2 * count]
    from_z = scratch[2 * count : 3 * count]
    w_buf, sums, rows_other = scratch[3 * count : 3 * count + 3]
    (w_sem, x_send, x_recv, c_send, c_recv, y_send, y_recv, z_send, z_recv) = scratch[3 * count + 3 :]
    half = rows_ref.shape[0] // 2
    quarter = half // 2
    span = line // groups
    chunk = quarter // span
    me = lax.axis_index("row")
    x = lax.axis_index("col")
    z, y, c = me // 4, lax.rem(me // 2, 2), lax.rem(me, 2)

    def row(z, y, c):
        return {"row": z * 4 + y * 2 + c}

    core_peer, y_peer = row(z, y, 1 - c), row(z, 1 - y, c)
    lower, upper = row(z - 1, y, c), row(z + 1, y, c)
    barrier = pltpu.get_barrier_semaphore()

    def greet(peer):
        pl.semaphore_signal(barrier, inc=1, device_id=peer, device_id_type=pl.DeviceIdType.MESH)

    greet(core_peer)
    greet(y_peer)
    if groups == 2:
        greet({"col": 1 - x})

    @pl.when(z > 0)
    def _():
        greet(lower)

    @pl.when(z < line - 1)
    def _():
        greet(upper)

    def load(k):
        low, high = pieces[k]
        return pltpu.make_async_copy(
            w_hbm.at[:, pl.ds(low, high - low)],
            w_buf.at[k % 2, :, pl.ds(0, high - low)],
            w_sem.at[k % 2],
        )

    for k in range(min(2, count)):
        load(k).start()
    pl.semaphore_wait(
        barrier, 1 + groups + jnp.where(z > 0, 1, 0) + jnp.where(z < line - 1, 1, 0)
    )

    def remote(src, dst, send, recv, peer):
        return pltpu.make_async_remote_copy(
            src_ref=src, dst_ref=dst, send_sem=send, recv_sem=recv,
            device_id=peer, device_id_type=pl.DeviceIdType.MESH,
        )

    if groups == 2:
        across = remote(rows_ref, rows_other, x_send.at[0], x_recv.at[0], {"col": 1 - x})
        across.start()
        across_whole = remote(
            g_hbm, g_other_hbm, x_send.at[1], x_recv.at[1], {"col": 1 - x}
        )

    if groups == 2 and count > 1:
        items = [(0, 0), (1, 0), (0, 1), (1, 1)]
        items += [(k, h) for k in range(2, count) for h in range(2)]
    else:
        items = [(k, h) for k in range(count) for h in range(groups)]

    def core_copy(i):
        k, h = items[i]
        width = pieces[k][1] - pieces[k][0]
        return remote(
            sums.at[i % 2, :, pl.ds(0, width)], held[k].at[h],
            c_send.at[i], c_recv.at[i], core_peer,
        )

    def y_copy(k, h):
        i = k * groups + h
        return remote(
            held[k].at[h, pl.ds(quarter, quarter), :], from_y[k].at[h],
            y_send.at[i], y_recv.at[i], y_peer,
        )

    def tiles(k, body):
        @pl.loop(0, (pieces[k][1] - pieces[k][0]) // unit)
        def _(i):
            body(pl.ds(pl.multiple_of(i * unit, unit), unit) if unit % 128 == 0 else slice(None))

    seen_w, seen_rows = set(), set([0])

    def send_sum(i):
        k, h = items[i]
        if k not in seen_w:
            seen_w.add(k)
            load(k).wait()
        if h not in seen_rows:
            seen_rows.add(h)
            across.wait_recv()
            across_whole.start()
        if i >= 2:
            core_copy(i - 2).wait_send()
        rows = rows_other if h else rows_ref

        def body(at):
            sums[i % 2, :, at] = jnp.dot(
                rows[pl.ds(half, half), :], w_buf[k % 2, :, at], preferred_element_type=jnp.float32
            )

        tiles(k, body)
        core_copy(i).start()

    def keep_sum(i):
        k, h = items[i]
        core_copy(i).wait_recv()
        rows = rows_other if h else rows_ref

        def body(at):
            held[k][h, :, at] += jnp.dot(
                rows[pl.ds(0, half), :], w_buf[k % 2, :, at], preferred_element_type=jnp.float32
            )

        tiles(k, body)
        y_copy(k, h).start()
        if h == groups - 1 and k + 2 < count:
            load(k + 2).start()

    def place(target):
        if groups == 2:
            return lax.rem(target // span + x, 2), lax.rem(target, span)
        return 0, target

    def z_copy(k, target, slot, peer):
        h, at = place(target)
        return remote(
            held[k].at[h, pl.ds(pl.multiple_of(at * chunk, chunk), chunk), :], from_z[k].at[slot],
            z_send.at[k, target], z_recv.at[k, slot], peer,
        )

    def add_arrived(k, target, slot):
        h, at = place(target)
        rows = pl.ds(pl.multiple_of(at * chunk, chunk), chunk)
        z_copy(k, target, slot, lower).wait_recv()
        held[k][h, rows, :] += from_z[k][slot]

    def rises(z, u):
        return z + u <= line - 1

    def take_y(k):
        for h in range(groups):
            y_copy(k, h).wait_recv()
            held[k][h, pl.ds(0, quarter), :] += from_y[k][h]

    def hop(k, u):
        @pl.when(rises(z, u))
        def _():
            @pl.when(z > 0)
            def _():
                add_arrived(k, z + u, z + u)

            z_copy(k, z + u, z + u, upper).start()

        @pl.when(z - u >= 0)
        def _():
            @pl.when(z < line - 1)
            def _():
                add_arrived(k, z - u, z - u)

            z_copy(k, z - u, line if u == 1 else z - u, lower).start()

    def finish(k):
        low, high = pieces[k]

        @pl.when(z > 0)
        def _():
            add_arrived(k, z, z)

        @pl.when(z < line - 1)
        def _():
            add_arrived(k, z, line)

        h, at = place(z)
        rows = pl.ds(pl.multiple_of(at * chunk, chunk), chunk)
        out_ref[:, low:high] = held[k][h, rows, :].astype(out_ref.dtype)

    def z_stage(n):
        for k in range(max(0, n - line), min(n, count - 1) + 1):
            if k == n:
                take_y(k)
            if n - k == line - 1:
                finish(k)
            elif n - k < line - 1:
                hop(k, line - 1 - (n - k))

    ahead = 0
    for i in range(len(items)):
        while ahead < len(items) and ahead <= i + 1:
            first_use = items[ahead][1] not in seen_rows or items[ahead][0] not in seen_w
            if ahead == i + 1 and first_use:
                break
            send_sum(ahead)
            ahead += 1
        keep_sum(i)
        k, h = items[i]
        if h == groups - 1 and k >= 2:
            z_stage(k - 2)
    for n in range(max(0, count - 2), count + line - 1):
        z_stage(n)

    if groups == 2:
        across.wait_send()
        across_whole.wait()
    for i in range(max(0, len(items) - 2), len(items)):
        core_copy(i).wait_send()
    for k in range(count):
        for h in range(groups):
            y_copy(k, h).wait_send()
        for target in range(line):

            @pl.when(z != target)
            def _():
                z_copy(k, target, target, lower).wait_send()


def reduce_of(rows, w_t, g_own, line, groups, seqs, block):
    hidden, width = w_t.shape
    pieces, unit = cuts(width)
    count = len(pieces)
    half = rows.shape[0] // 2
    widest = max(high - low for low, high in pieces)
    widths = [high - low for low, high in pieces]
    chunk = seqs * block
    dma = pltpu.SemaphoreType.DMA
    anywhere = pl.BlockSpec(memory_space=pl.ANY)
    whole = [g_own] if groups == 2 else []
    scratch = [pltpu.VMEM((groups, half, n), jnp.float32) for n in widths]
    scratch += [pltpu.VMEM((groups, half // 2, n), jnp.float32) for n in widths]
    scratch += [pltpu.VMEM((line + 1, chunk, n), jnp.float32) for n in widths]
    scratch += [
        pltpu.VMEM((2, hidden, widest), jnp.bfloat16),
        pltpu.VMEM((2, half, widest), jnp.float32),
        pltpu.VMEM((2 * half if groups == 2 else 16, hidden), jnp.bfloat16),
        dma((2,)), dma((2,)), dma((2,)),
        dma((groups * count,)), dma((groups * count,)),
        dma((groups * count,)), dma((groups * count,)),
        dma((count, line)), dma((count, line + 1)),
    ]
    return pl.pallas_call(
        lambda *refs: reduce_kernel(line, groups, pieces, unit, *refs),
        out_shape=[jax.ShapeDtypeStruct((chunk, width), jnp.bfloat16)]
        + [jax.ShapeDtypeStruct(g.shape, g.dtype) for g in whole],
        in_specs=[pl.BlockSpec(memory_space=pltpu.VMEM), anywhere] + [anywhere for _ in whole],
        out_specs=[pl.BlockSpec(memory_space=pltpu.VMEM)] + [anywhere for _ in whole],
        scratch_shapes=scratch,
        cost_estimate=pl.CostEstimate(
            flops=4 * groups * half * hidden * width * 2,
            bytes_accessed=2 * hidden * width,
            transcendentals=0,
        ),
        compiler_params=pltpu.CompilerParams(
            collective_id=0, has_side_effects=True, vmem_limit_bytes=60 * 2**20
        ),
    )(rows, w_t, *whole)


def make_local(n_row, n_col):
    line = n_row // 4

    def local(activations, output_gradient, weight):
        seqs, own, hidden = output_gradient.shape
        width = weight.shape[0]
        me = lax.axis_index("row")
        y, c = (me // 2) % 2, me % 2
        act = lax.all_gather(activations, "row", axis=1, tiled=True)
        g_own = jnp.swapaxes(output_gradient, 1, 2)
        groups = 2 if n_col == 2 and line % 2 == 0 else 1
        if groups == 2:
            group = output_gradient
        else:
            g_t = lax.all_gather(g_own, "col", axis=2, tiled=True)
            group = jnp.swapaxes(g_t, 1, 2)
        block = own * n_col // n_row

        span = line // groups
        g = group.reshape(seqs, span, 2, 2, block, hidden).transpose(3, 2, 1, 0, 4, 5)
        g = jnp.where(c == 0, g, g[::-1])
        g = jnp.where(y == 0, g, g[:, ::-1])
        rows = g.reshape(4 * span * seqs * block, hidden)
        grad, *others = reduce_of(rows, weight.T, g_own, line, groups, seqs, block)
        if groups == 2:
            first = lax.axis_index("col") == 0
            g_t = jnp.concatenate(
                [jnp.where(first, g_own, others[0]), jnp.where(first, others[0], g_own)], axis=2
            )
        return fisher_of(g_t, act).T, grad.reshape(seqs, block, width)

    return local


def solution(mesh):
    return jax.shard_map(
        make_local(mesh.shape["row"], mesh.shape["col"]),
        mesh=mesh,
        in_specs=(P(None, "row", "col"), P(None, "col", "row"), P("col", "row")),
        out_specs=(P("col", "row"), P(None, "row", "col")),
        check_vma=False,
    )
```

time: 482 us -> 327 us (0.68)
  waiting for transfers between devices: 315 us -> 0.68 us
  Pallas kernels: 0 us -> 299 us
  matrix products: 113 us -> 0 us
  other arithmetic: 39.9 us -> 4.66 us
  local copies, waits for them, and re-layouts: 0 us -> 7.28 us
    pallas_call x0 -> x2, Pallas kernels: none -> 299 us  [the longest x1 259 us: reduce_of(): pl.pallas_call(lambda *refs: reduce_kernel(line, groups, pieces, unit, *r...]
    reduce_scatter x1 -> x0, waiting for transfers between devices: 178 us -> none  [local(): lax.psum_scatter(partial_totals, 'row', scatter_dimension=1, tiled=True)]
    all_gather x2 -> x1, waiting for transfers between devices: 135 us -> 0.01 us  [local(): act = lax.all_gather(activations, 'row', axis=1, tiled=True)]
    dot_general x2 -> x0, matrix products: 113 us -> none  [the longest x1 72.8 us: local(): jnp.einsum('qkc,qkh->qch', input_gathered, gradient_everything, preferred...]
    div x1 -> x0, other arithmetic: 37.4 us -> none  [local(): fisher = jnp.sum(gradient_list * gradient_list, axis=0) / (seqs * length)]
    unnamed x0 -> x8, local copies, waits for them, and re-layouts: none -> 5.8 us
  transfers between devices with their start and end apart: 3 -> 1, of which waited for: 3 -> 0; matrix products, arithmetic and copies ran while one was open for 31% -> 3% of each run, Pallas kernels for 0% -> 79%
where the time goes in v1:
time: 327 us; the launch traced here: 326 us
  Pallas kernels  299 us (91%)
  between operations  14.1 us (4%)
  local copies, waits for them, and re-layouts  7.28 us (2%)
  other arithmetic  4.66 us (1%)
    pallas_call x1, Pallas kernels, reduce_of(): pl.pallas_call(lambda *refs: reduce_kernel(line, groups, pieces, unit, *r...  259 us
    pallas_call x1, Pallas kernels, fisher_of(): pl.pallas_call(lambda *refs: fisher_kernel(1.0 / (seqs * length), *refs),...  40.6 us
  transfers between devices with their start and end apart: 1, of which 0 were waited for; matrix products, arithmetic and copies ran while one was open for 3% of the time, Pallas kernels for 79%

profile of v1, /device:TPU:0, one launch (start us, length us, event | category | flops | bytes accessed | tf_op | source)
XLA Modules:
  0.0 326.0 jit_solution(5116723589886715295)
XLA Ops:
  7.2 0.0 all-gather.2.cloned.1.call-start
  7.2 0.7 all-gather.2.cloned.1.call-update
  7.9 2.8 copy.6
  10.7 0.3 reverse_select_fusion.1
  11.1 0.4 reverse_select_fusion
  11.4 1.5 copy.7
  12.9 0.0 copy-start.1
  12.9 258.6 %shard_map.50 = (bf16[64,7424]{1,0:T(8,128)(2,1)}, bf16[2,1856,256]{2,1,0:T(8,128)(2,1)}) custom-call(bf16[512,1856]{1,0:T(8,128)(2,1)} %bitcast.12, bf16[1856,7424]{1,0:T(8,128)(2,1)} %bitcast.14, bf16[2,1856,256]{2,1,0:T(8,128)(2,1)} %bitcast.11), custom_call_target="tpu_custom_call" | custom-call | flops 56438554624 | bytes 27557888 | tf_op jit(solution)/shard_map/pallas_call | solution.py:306
  271.6 0.0 copy-done.1
  271.6 1.8 broadcast_select_fusion.1
  273.4 2.2 pad_maximum_fusion.refs_0_
  275.5 0.0 all-gather.2.cloned.1.call-done.refs_1_
  275.6 0.0 copy-start
  275.6 2.1 copy-done
  277.6 0.0 copy-start.2
  277.6 40.6 %shard_map.51 = f32[1856,7424]{1,0:T(8,128)} custom-call(bf16[2,1856,512]{2,1,0:T(8,128)(2,1)S(1)} %copy-done, bf16[2,512,7424]{2,1,0:T(8,128)(2,1)} %all-gather.2.cloned.1.call-done.refs_1_), custom_call_target="tpu_custom_call" | custom-call | flops 28219277312 | bytes 74121216 | tf_op jit(solution)/shard_map/pallas_call | solution.py:28
  318.2 0.0 copy-done.2
  318.2 0.9 copy.9
Async XLA Ops:
  7.2 268.4 %all-gather.2.cloned.1.call-start = ((), (), s32[]{:S(2)}) async-start(), calls=%async_computation | async-start | bytes 16154624 | tf_op jit(solution)/shard_map/all_gather | solution.py:332
  12.9 258.7 %copy-start.1 = (bf16[2,256,1856]{1,2,0:T(8,128)(2,1)S(1)}, bf16[2,256,1856]{1,2,0:T(8,128)(2,1)}, u32[]{:S(2)}) copy-start(bf16[2,256,1856]{1,2,0:T(8,128)(2,1)} %param.4) | copy-start | bytes 5701636
  275.6 2.1 copy-start
  277.6 40.6 %copy-start.2 = (bf16[64,7424]{1,0:T(8,128)(2,1)S(1)}, bf16[64,7424]{1,0:T(8,128)(2,1)}, u32[]{:S(2)}) copy-start(bf16[64,7424]{1,0:T(8,128)(2,1)} %get-tuple-element.5) | copy-start | bytes 2850820
Sparse Core Ops, SparseCore 0:
  10.3 175.7 all-gather.1
